TPU v7x, 128 devices: a whole 4x4x4 slice. The times are simulated.
128 devices in a mesh: dp: 32 (over z, y, x_hi), tensor: 4 (over x_lo, core).
Axes of the slice: x: 4 (x_hi: 2, x_lo: 2; x = x_hi * 2 + x_lo), y: 4, z: 4, core: 2. Of those that a mesh axis runs over, the one named last changes fastest.
Arguments:
- block_input: bfloat16 [32768, 1024], P(('dp', 'tensor')), may hold values from -6 to 6
- positions: int32 [32768], P('dp'), may hold values from 0 to 1021, as said below
- attn_gain: float32 [1024], replicated, may hold values from 0.1 to 1.9
- w_query: bfloat16 [1024, 1024], P('dp', 'tensor'), may hold values from -0.1875 to 0.1875
- w_key: bfloat16 [1024, 512], P('dp', 'tensor'), may hold values from -0.1875 to 0.1875
- w_value: bfloat16 [1024, 512], P('dp', 'tensor'), may hold values from -0.1875 to 0.1875
- w_output: bfloat16 [1024, 1024], P('tensor', 'dp'), may hold values from -0.75 to 0.75
- q_gain: float32 [64], replicated, may hold values from 0.7 to 2
- k_gain: float32 [64], replicated, may hold values from 0.7 to 2
- ffn_gain: float32 [1024], replicated, may hold values from 0.1 to 1.9
- w_gate: bfloat16 [1024, 4608], P('dp', 'tensor'), may hold values from -0.1875 to 0.1875
- w_up: bfloat16 [1024, 4608], P('dp', 'tensor'), may hold values from -0.1875 to 0.1875
- w_down: bfloat16 [4608, 1024], P('tensor', 'dp'), may hold values from -0.09375 to 0.09375
- cotangent: bfloat16 [32768, 1024], P(('dp', 'tensor')), may hold values from -6 to 6
Outputs:
- layer_output: bfloat16 [32768, 1024], P(('dp', 'tensor'))
- input_grad: float32 [32768, 1024], P(('dp', 'tensor'))
- attn_gain_grad: float32 [1024], replicated
- query_weight_grad: float32 [1024, 1024], P('dp', 'tensor')
- key_weight_grad: float32 [1024, 512], P('dp', 'tensor')
- value_weight_grad: float32 [1024, 512], P('dp', 'tensor')
- output_weight_grad: float32 [1024, 1024], P('tensor', 'dp')
- q_gain_grad: float32 [64], replicated
- k_gain_grad: float32 [64], replicated
- ffn_gain_grad: float32 [1024], replicated
- gate_weight_grad: float32 [1024, 4608], P('dp', 'tensor')
- up_weight_grad: float32 [1024, 4608], P('dp', 'tensor')
- down_weight_grad: float32 [4608, 1024], P('tensor', 'dp')
Inputs may be any that keep to these rules, and one draw needn't show every extreme that they name: Within each sequence of 1024 tokens positions count up by one and fall back to 0 where a document starts; each sequence holds three documents, the middle one starting within the first 256 tokens and ending within the last 256; in one sequence the middle document starts at row 1 and ends at row 1022.
All inputs are finite; a program needn't handle non-finite values.
Results may differ from a plain program's by a relative error of at most 0.025.
Values may be sent and summed in bfloat16 or wider, within the bound.
A program may use at most 128 MiB of HBM per device.

v0:
```python
import functools
import math

import jax
import jax.numpy as jnp
from jax import lax
from jax.experimental import pallas as pl
from jax.experimental.pallas import tpu as pltpu
from jax.sharding import PartitionSpec as P

epsilon = 1e-05
rope_base = 1000000.0
f32 = jnp.float32
bf16 = jnp.bfloat16
MESH = pl.DeviceIdType.MESH
VMEM_SPEC = pl.BlockSpec(memory_space=pltpu.VMEM)
VMEM_LIMIT = 60 * 1024 * 1024


class Place:
    def __init__(self):
        d = lax.axis_index("dp")
        t = lax.axis_index("tensor")
        self.z = lax.div(d, 8)
        self.y = lax.rem(lax.div(d, 2), 4)
        self.h = lax.rem(d, 2)
        self.xl = lax.div(t, 2)
        self.core = lax.rem(t, 2)
        self.d = d
        self.t = t

    def at(self, dz=0, dy=0, dh=0):
        z = lax.rem(self.z + (dz + 4), 4)
        y = lax.rem(self.y + (dy + 4), 4)
        h = self.h if dh == 0 else 1 - self.h
        return z * 8 + y * 2 + h

    def dp_device(self, dz=0, dy=0, dh=0):
        return (self.at(dz, dy, dh), self.t)

    def core_device(self):
        return (self.d, self.xl * 2 + (1 - self.core))

    def x_device(self):
        return (self.d, (1 - self.xl) * 2 + self.core)

    def token_block(self, dx=0, dc=0):
        xl = self.xl if dx == 0 else 1 - self.xl
        core = self.core if dc == 0 else 1 - self.core
        return xl * 2 + core


def greet(devices):
    barrier = pltpu.get_barrier_semaphore()
    for device in devices:
        pl.semaphore_signal(barrier, inc=1, device_id=device, device_id_type=MESH)
    pl.semaphore_wait(barrier, len(devices))


def ring_devices(me):
    return [
        me.dp_device(dz=1),
        me.dp_device(dz=-1),
        me.dp_device(dy=1),
        me.dp_device(dy=-1),
        me.dp_device(dh=1),
    ]


def remote(src, dst, send, recv, index, device):
    return pltpu.make_async_remote_copy(
        src_ref=src,
        dst_ref=dst,
        send_sem=send.at[index],
        recv_sem=recv.at[index],
        device_id=device,
        device_id_type=MESH,
    )


def offsets(kind, first, second):
    return (first, second) if kind == 0 else (second, first)


class WeightGather:
    COUNT = 41

    def __init__(self, me, full, send, recv):
        self.me, self.full, self.send, self.recv = me, full, send, recv
        self.started = []

    def block(self, kind, first, second, part=None):
        dz, dy = offsets(kind, first, second)
        row = self.me.at(dz, dy, kind) * 32
        if part is None:
            return self.full.at[pl.ds(pl.multiple_of(row, 32), 32)]
        return self.full.at[pl.ds(pl.multiple_of(row + part * 16, 16), 16)]

    def push(self, ref, index, device):
        copy = remote(ref, ref, self.send, self.recv, index, device)
        copy.start()
        self.started.append(copy)

    def arrived(self, ref, index):
        remote(ref, ref, self.send, self.recv, index, self.me.dp_device(dh=1)).wait_recv()

    def along(self, kind, level, step):
        dz, dy = offsets(kind, step, 0) if level == 0 else offsets(kind, 0, step)
        return self.me.dp_device(dz=dz, dy=dy)

    def base(self, kind, level, chunk):
        return 1 + kind * 4 + chunk * 0 if level == 0 else 9 + kind * 16 + chunk * 4

    def spread(self, kind, level, chunk):
        first = (0, -1, 1, 2)[chunk] if level == 1 else 0
        base = self.base(kind, level, chunk)
        ref = self.block(kind, first, 0)
        self.push(ref, base, self.along(kind, level, 1))
        self.push(ref, base + 1, self.along(kind, level, -1))

    def pass_on(self, kind, level, chunk, side):
        first = (0, -1, 1, 2)[chunk] if level == 1 else 0
        base = self.base(kind, level, chunk)
        step = -1 if side == 0 else 1
        where = (step, 0) if level == 0 else (first, step)
        self.arrived(self.block(kind, *where), base + side)
        self.push(self.block(kind, *where, part=side), base + 2 + side, self.along(kind, level, -step))

    def last(self, kind, level, chunk):
        first = (0, -1, 1, 2)[chunk] if level == 1 else 0
        base = self.base(kind, level, chunk)
        where = (2, 0) if level == 0 else (first, 2)
        for side in range(2):
            self.arrived(self.block(kind, *where, part=side), base + 2 + side)

    def begin(self):
        self.push(self.block(0, 0, 0), 0, self.me.dp_device(dh=1))
        self.spread(0, 0, 0)
        self.spread(0, 1, 0)

    def step1(self):
        self.arrived(self.block(1, 0, 0), 0)
        self.spread(1, 0, 0)
        self.spread(1, 1, 0)

    def step2(self):
        for kind in range(2):
            for side in range(2):
                self.pass_on(kind, 0, 0, side)
                self.spread(kind, 1, 1 + side)

    def step3(self):
        for kind in range(2):
            self.last(kind, 0, 0)
            self.spread(kind, 1, 3)

    def step4(self):
        for chunk in range(4):
            for kind in range(2):
                for side in range(2):
                    self.pass_on(kind, 1, chunk, side)

    def finish(self):
        for chunk in range(4):
            for kind in range(2):
                self.last(kind, 1, chunk)
        for copy in self.started:
            copy.wait_send()


class TokenGather:
    COUNT = 12
    CHUNKS = 4
    ROWS = 64

    def __init__(self, me, rows, send, recv):
        self.me, self.rows, self.send, self.recv = me, rows, send, recv
        self.started = []

    def piece(self, dx, dc, chunk):
        row = self.me.token_block(dx, dc) * 256 + chunk * self.ROWS
        return self.rows.at[pl.ds(pl.multiple_of(row, self.ROWS), self.ROWS)]

    def push(self, ref, index, device):
        copy = remote(ref, ref, self.send, self.recv, index, device)
        copy.start()
        self.started.append(copy)

    def arrived(self, ref, index):
        remote(ref, ref, self.send, self.recv, index, self.me.core_device()).wait_recv()

    def begin(self, chunk):
        own = self.piece(0, 0, chunk)
        self.push(own, chunk, self.me.x_device())
        self.push(own, 4 + chunk, self.me.core_device())

    def pass_on(self, chunk):
        other = self.piece(1, 0, chunk)
        self.arrived(other, chunk)
        self.push(other, 8 + chunk, self.me.core_device())

    def finish(self):
        for chunk in range(self.CHUNKS):
            self.arrived(self.piece(0, 1, chunk), 4 + chunk)
        for chunk in range(self.CHUNKS):
            self.arrived(self.piece(1, 1, chunk), 8 + chunk)
        for copy in self.started:
            copy.wait_send()


class TokenScatter:
    COUNT = 12
    CHUNKS = 4
    ROWS = 64

    def __init__(self, me, part, near, far, relay, send, recv):
        self.me, self.part, self.near, self.far, self.relay = me, part, near, far, relay
        self.send, self.recv = send, recv
        self.started = []

    def piece(self, dx, dc, chunk):
        row = self.me.token_block(dx, dc) * 256 + chunk * self.ROWS
        return pl.ds(pl.multiple_of(row, self.ROWS), self.ROWS)

    def push(self, src, dst, index, device):
        copy = remote(src, dst, self.send, self.recv, index, device)
        copy.start()
        self.started.append(copy)

    def arrived(self, ref, index):
        remote(ref, ref, self.send, self.recv, index, self.me.core_device()).wait_recv()

    def begin_far(self, chunk):
        self.push(
            self.part.at[self.piece(1, 1, chunk)], self.relay.at[chunk], chunk, self.me.core_device()
        )

    def begin_near(self, chunk):
        self.push(
            self.part.at[self.piece(0, 1, chunk)], self.near.at[chunk], 4 + chunk, self.me.core_device()
        )

    def relay_on(self, chunk):
        self.arrived(self.relay.at[chunk], chunk)
        total = self.relay[chunk].astype(f32) + self.part[self.piece(1, 0, chunk), :].astype(f32)
        self.relay[chunk] = total.astype(bf16)
        self.push(self.relay.at[chunk], self.far.at[chunk], 8 + chunk, self.me.x_device())

    def total(self, chunk):
        self.arrived(self.near.at[chunk], 4 + chunk)
        self.arrived(self.far.at[chunk], 8 + chunk)
        return (
            self.part[self.piece(0, 0, chunk), :].astype(f32)
            + self.near[chunk].astype(f32)
            + self.far[chunk].astype(f32)
        )

    def finish(self):
        for copy in self.started:
            copy.wait_send()


def scatter_scratch():
    return [pltpu.VMEM((4, 64, 1024), bf16)] * 3 + [pltpu.SemaphoreType.DMA((12,))] * 2


class GradScatter:
    COUNT = 61

    def __init__(self, me, part, recv_half, recv_full, out_half, sums, last, send, recv):
        self.me, self.part = me, part
        self.recv_half, self.recv_full = recv_half, recv_full
        self.out_half, self.sums, self.last = out_half, sums, last
        self.send, self.recv = send, recv
        self.started = []

    def rows(self, kind, first, second, part=None):
        dz, dy = offsets(kind, first, second)
        row = self.me.at(dz, dy, kind) * 32
        if part is None:
            return pl.ds(pl.multiple_of(row, 32), 32)
        return pl.ds(pl.multiple_of(row + part * 16, 16), 16)

    def push(self, src, dst, index, device):
        copy = remote(src, dst, self.send, self.recv, index, device)
        copy.start()
        self.started.append(copy)

    def arrived(self, ref, index):
        remote(ref, ref, self.send, self.recv, index, self.me.dp_device(dh=1)).wait_recv()

    def along(self, kind, level, step):
        dz, dy = offsets(kind, step, 0) if level == 0 else offsets(kind, 0, step)
        return self.me.dp_device(dz=dz, dy=dy)

    def slot(self, kind, level, chunk):
        return kind * 5 + (4 if level == 0 else chunk)

    def source(self, kind, level, chunk, offset):
        if level == 1:
            first = (0, -1, 1, 2)[chunk]
            return self.part, self.rows(kind, first, offset), [
                self.rows(kind, first, offset, part) for part in range(2)
            ]
        chunk = {0: 0, -1: 1, 1: 2, 2: 3}[offset]
        base = (kind * 4 + chunk) * 32
        return self.sums, pl.ds(base, 32), [pl.ds(base, 16), pl.ds(base + 16, 16)]

    def far(self, kind, level, chunk):
        slot = self.slot(kind, level, chunk)
        ref, _, halves = self.source(kind, level, chunk, 2)
        self.push(ref.at[halves[0]], self.recv_half.at[slot, 0], slot * 6, self.along(kind, level, 1))
        self.push(
            ref.at[halves[1]], self.recv_half.at[slot, 1], slot * 6 + 1, self.along(kind, level, -1)
        )

    def near(self, kind, level, chunk):
        slot = self.slot(kind, level, chunk)
        for side in range(2):
            step = 1 if side == 0 else -1
            ref, _, halves = self.source(kind, level, chunk, step)
            self.push(
                ref.at[halves[1 - side]],
                self.recv_full.at[slot, side, pl.ds(16 * (1 - side), 16)],
                slot * 6 + 4 + side,
                self.along(kind, level, step),
            )

    def middle(self, kind, level, chunk, side):
        slot = self.slot(kind, level, chunk)
        step = 1 if side == 0 else -1
        ref, _, halves = self.source(kind, level, chunk, step)
        self.arrived(self.recv_half.at[slot, side], slot * 6 + side)
        total = ref[halves[side], :].astype(f32) + self.recv_half[slot, side].astype(f32)
        self.out_half[slot, side] = total.astype(bf16)
        self.push(
            self.out_half.at[slot, side],
            self.recv_full.at[slot, side, pl.ds(16 * side, 16)],
            slot * 6 + 2 + side,
            self.along(kind, level, step),
        )

    def total(self, kind, level, chunk):
        slot = self.slot(kind, level, chunk)
        ref, whole, _ = self.source(kind, level, chunk, 0)
        for side in range(2):
            full = self.recv_full.at[slot, side]
            self.arrived(full.at[pl.ds(16 * side, 16)], slot * 6 + 2 + side)
            self.arrived(full.at[pl.ds(16 * (1 - side), 16)], slot * 6 + 4 + side)
        return (
            ref[whole, :].astype(f32)
            + self.recv_full[slot, 0].astype(f32)
            + self.recv_full[slot, 1].astype(f32)
        )

    def begin(self):
        for push in (self.far, self.near):
            for chunk in range(4):
                for kind in range(2):
                    push(kind, 1, chunk)

    def step1(self, chunk):
        for kind in range(2):
            for side in range(2):
                self.middle(kind, 1, chunk, side)

    def step2(self, chunk):
        for kind in range(2):
            total = self.total(kind, 1, chunk)
            self.sums[pl.ds((kind * 4 + chunk) * 32, 32), :] = total.astype(bf16)

    def step3(self):
        for push in (self.far, self.near):
            for kind in range(2):
                push(kind, 0, 0)

    def step4(self):
        for kind in (1, 0):
            for side in range(2):
                self.middle(kind, 0, 0, side)

    def step5(self):
        self.last[0] = self.total(1, 0, 0).astype(bf16)
        self.push(self.last.at[0], self.last.at[1], 60, self.me.dp_device(dh=1))

    def result(self):
        own = self.total(0, 0, 0)
        self.arrived(self.last.at[1], 60)
        return own + self.last[1].astype(f32)

    def finish(self):
        for copy in self.started:
            copy.wait_send()


def grad_scratch(width):
    return [
        pltpu.VMEM((10, 2, 16, width), bf16),
        pltpu.VMEM((10, 2, 32, width), bf16),
        pltpu.VMEM((10, 2, 16, width), bf16),
        pltpu.VMEM((256, width), bf16),
        pltpu.VMEM((2, 32, width), bf16),
        pltpu.SemaphoreType.DMA((61,)),
        pltpu.SemaphoreType.DMA((61,)),
    ]


def row_scale(values):
    return lax.rsqrt(jnp.mean(values * values, axis=-1, keepdims=True) + epsilon)


def norm_back(values, inverse, gain_vec, upstream):
    weighted = upstream * gain_vec
    row_inner = jnp.mean(weighted * values, axis=-1, keepdims=True)
    return inverse * weighted - values * inverse * inverse * inverse * row_inner


def call(kernel, outs, scratch, number, args, flops=0, moved=0):
    return pl.pallas_call(
        kernel,
        out_shape=outs,
        in_specs=[VMEM_SPEC] * len(args),
        out_specs=[VMEM_SPEC] * len(outs),
        scratch_shapes=scratch,
        cost_estimate=pl.CostEstimate(flops=flops, bytes_accessed=moved, transcendentals=0),
        compiler_params=pltpu.CompilerParams(
            collective_id=number, has_side_effects=True, vmem_limit_bytes=VMEM_LIMIT
        ),
    )(*args)


def dot(a, b):
    return jnp.dot(a, b, preferred_element_type=f32)


def dot_tb(a, b):
    return lax.dot_general(a, b, (((1,), (1,)), ((), ())), preferred_element_type=f32)


def head_scale(values):
    return lax.rsqrt(jnp.mean(values * values, axis=0, keepdims=True) + epsilon)


def rotate(values, cosine, sine):
    front, back = values[:32], values[32:]
    return jnp.concatenate([front * cosine - back * sine, back * cosine + front * sine], axis=0)


def rotate_back(values, cosine, sine):
    front, back = values[:32], values[32:]
    return jnp.concatenate([front * cosine + back * sine, back * cosine - front * sine], axis=0)


def project_block(block, rows_ref, weight_ref, pre_ref, low):
    here = pl.ds(pl.multiple_of(block * 256, 256), 256)
    flat = dot(rows_ref[here, :], weight_ref[:, 0:512])
    turned = flat.T
    pre_ref[:, here] = turned[:384]
    cosine, sine = low.cos[:, here], low.sin[:, here]
    for head in range(4):
        u = turned[64 * head : 64 * head + 64]
        u = u * head_scale(u) * low.q_gain[...]
        low.q[pl.ds(64 * head, 64), here] = (rotate(u, cosine, sine) * 0.125).astype(bf16)
    for head in range(2):
        u = turned[256 + 64 * head : 320 + 64 * head]
        u = rotate(u * head_scale(u) * low.k_gain[...], cosine, sine)
        low.kt[head, block] = u.astype(bf16)
        low.k[head, here, :] = u.T.astype(bf16)
        u = turned[384 + 64 * head : 448 + 64 * head]
        low.vt[head, block, 0:64, :] = u.astype(bf16)
        low.vt[head, block, 64:80, :] = jnp.ones((16, 256), bf16)
        low.v[head, here, :] = u.T.astype(bf16)


def pair_lanes(ref, head, here):
    return jnp.concatenate(
        [ref[pl.ds(128 * head, 64), here], ref[pl.ds(128 * head + 64, 64), here]], axis=1
    )


def seen(low, number, key_block, diagonal):
    here = pl.ds(number * 256, 256)
    key_row = lax.broadcasted_iota(jnp.int32, (256, 256), 0) + key_block * 256
    mask = key_row >= low.start[:, here]
    if diagonal:
        query_row = lax.broadcasted_iota(jnp.int32, (256, 256), 1) + number * 256
        mask = jnp.logical_and(mask, key_row <= query_row)
    return jnp.concatenate([mask, mask], axis=1)


def forward_block(low, head, number, acc):
    here = pl.ds(number * 256, 256)
    queries = pair_lanes(low.q, head, here)

    def step(key_block, diagonal):
        keys = low.k[head, pl.ds(pl.multiple_of(key_block * 256, 256), 256), :]
        weight = jnp.exp(dot(keys, queries))
        weight = jnp.where(seen(low, number, key_block, diagonal), weight, 0.0).astype(bf16)
        return dot(low.vt[head, key_block], weight)

    acc[...] = step(number, True)
    if number > 0:

        @pl.loop(0, number)
        def _(key_block):
            acc[...] += step(key_block, False)

    total = acc[64:65, :]
    mixed = acc[0:64, :] / total
    low.lse[2 * head : 2 * head + 1, here] = jnp.log(total[:, 0:256])
    low.lse[2 * head + 1 : 2 * head + 2, here] = jnp.log(total[:, 256:512])
    low.mixed[pl.ds(128 * head, 64), here] = mixed[:, 0:256]
    low.mixed[pl.ds(128 * head + 64, 64), here] = mixed[:, 256:512]


def backward_prepare(block, rows_ref, weight_ref, low):
    here = pl.ds(pl.multiple_of(block * 256, 256), 256)
    turned = dot(rows_ref[here, :], weight_ref[:, 512:768]).T.astype(bf16)
    low.gt[:, here] = turned
    for head in range(4):
        part = turned[64 * head : 64 * head + 64].astype(f32)
        low.g[head, here, :] = part.T.astype(bf16)
        mixed = low.mixed[pl.ds(64 * head, 64), here]
        low.inner[head : head + 1, here] = jnp.sum(part * mixed, axis=0, keepdims=True)
        low.qn[head, here, :] = low.q[pl.ds(64 * head, 64), here].astype(f32).T.astype(bf16)


def backward_block(low, head, number, acc):
    here = pl.ds(number * 256, 256)
    queries = pair_lanes(low.q, head, here)
    upstream = pair_lanes(low.gt, head, here)
    query_rows = jnp.concatenate([low.qn[2 * head, here, :], low.qn[2 * head + 1, here, :]], axis=0)
    upstream_rows = jnp.concatenate([low.g[2 * head, here, :], low.g[2 * head + 1, here, :]], axis=0)

    def both(ref):
        return jnp.concatenate(
            [ref[2 * head : 2 * head + 1, here], ref[2 * head + 1 : 2 * head + 2, here]], axis=1
        )

    lse = both(low.lse)
    inner = both(low.inner)

    def step(key_block, diagonal):
        rows = pl.ds(pl.multiple_of(key_block * 256, 256), 256)
        weight = jnp.exp(dot(low.k[head, rows, :], queries) - lse)
        weight = jnp.where(seen(low, number, key_block, diagonal), weight, 0.0)
        score = weight * (dot(low.v[head, rows, :], upstream) - inner)
        score = score.astype(bf16)
        value_part = dot(weight.astype(bf16), upstream_rows)
        key_part = dot(score, query_rows)
        if diagonal:
            low.dv[head, rows, :] = value_part
            low.dk[head, rows, :] = key_part
        else:
            low.dv[head, rows, :] += value_part
            low.dk[head, rows, :] += key_part
        return dot(low.kt[head, key_block], score)

    acc[0:64, :] = step(number, True)
    if number > 0:

        @pl.loop(0, number)
        def _(key_block):
            acc[0:64, :] += step(key_block, False)

    low.dq[pl.ds(128 * head, 64), here] = acc[0:64, 0:256]
    low.dq[pl.ds(128 * head + 64, 64), here] = acc[0:64, 256:512]


def head_norm_back(values, gain, upstream):
    inverse = head_scale(values)
    weighted = upstream * gain
    inner = jnp.mean(weighted * values, axis=0, keepdims=True)
    return inverse * weighted - values * inverse * inverse * inverse * inner, inverse


def backward_finish(block, low, pre_ref, turned_ref, flat_ref):
    here = pl.ds(pl.multiple_of(block * 256, 256), 256)
    cosine, sine = low.cos[:, here], low.sin[:, here]
    q_part = jnp.zeros((64, 1), f32)
    k_part = jnp.zeros((64, 1), f32)
    for head in range(4):
        rows = pl.ds(64 * head, 64)
        upstream = rotate_back(low.dq[rows, here] * 0.125, cosine, sine)
        values = pre_ref[rows, here]
        grad, inverse = head_norm_back(values, low.q_gain[...], upstream)
        q_part = q_part + jnp.sum(upstream * values * inverse, axis=1, keepdims=True)
        turned_ref[rows, here] = grad.astype(bf16)
    for head in range(2):
        rows = pl.ds(256 + 64 * head, 64)
        upstream = rotate_back(low.dk[head, here, :].T, cosine, sine)
        values = pre_ref[rows, here]
        grad, inverse = head_norm_back(values, low.k_gain[...], upstream)
        k_part = k_part + jnp.sum(upstream * values * inverse, axis=1, keepdims=True)
        turned_ref[rows, here] = grad.astype(bf16)
        turned_ref[pl.ds(384 + 64 * head, 64), here] = low.dv[head, here, :].T.astype(bf16)
    flat_ref[here, :] = turned_ref[:, here].astype(f32).T.astype(bf16)
    return q_part, k_part


class GainSum:
    def __init__(self, me, row, plane, send, recv):
        self.me, self.row, self.plane = me, row, plane
        self.send, self.recv = send, recv
        self.started = []

    def row_devices(self):
        me = self.me
        return [
            (me.at(dh=step // 4), lax.rem(me.t + step % 4, 4)) for step in range(1, 8)
        ]

    def plane_devices(self):
        return [self.me.dp_device(dz=step // 4, dy=step % 4) for step in range(1, 16)]

    def exchange(self, slots, place, value, devices, base):
        slots[place] = value
        for step, device in enumerate(devices):
            copy = remote(
                slots.at[place], slots.at[place], self.send, self.recv, base + step, device
            )
            copy.start()
            self.started.append(copy)
        for step, device in enumerate(devices):
            remote(
                slots.at[place], slots.at[place], self.send, self.recv, base + step, device
            ).wait_recv()
        total = slots[0]
        for slot in range(1, len(devices) + 1):
            total = total + slots[slot]
        return total

    def run(self, value):
        me = self.me
        value = self.exchange(self.row, me.h * 4 + me.t, value, self.row_devices(), 0)
        value = self.exchange(self.plane, me.z * 4 + me.y, value, self.plane_devices(), 7)
        for copy in self.started:
            copy.wait_send()
        return value


def gain_scratch():
    return [
        pltpu.VMEM((8, 24, 128), f32),
        pltpu.VMEM((16, 24, 128), f32),
        pltpu.SemaphoreType.DMA((22,)),
        pltpu.SemaphoreType.DMA((22,)),
    ]


class Fields:
    def __init__(self, **refs):
        self.__dict__.update(refs)


def gather_services(gather):
    steps = [gather.step1]
    for kind in range(2):
        for side in range(2):

            def hand_on(kind=kind, side=side):
                gather.pass_on(kind, 0, 0, side)
                gather.spread(kind, 1, 1 + side)

            steps.append(hand_on)
    steps.append(gather.step3)
    for chunk in range(4):

        def hand_bulk(chunk=chunk):
            for kind in range(2):
                for side in range(2):
                    gather.pass_on(kind, 1, chunk, side)

        steps.append(hand_bulk)
    return steps


def column(row_ref):
    return jnp.broadcast_to(row_ref[...], (128, 64)).T[:, 0:1]


def tables(position_ref, q_gain_ref, k_gain_ref, cos, sin, start, q_gain, k_gain):
    place = lax.broadcasted_iota(jnp.int32, (32, 1024), 0).astype(f32)
    frequency = jnp.exp(place * (-math.log(rope_base) * 2.0 / 64))
    angles = frequency * position_ref[...].astype(f32)
    cos[...] = jnp.cos(angles)
    sin[...] = jnp.sin(angles)
    start[...] = lax.broadcasted_iota(jnp.int32, (1, 1024), 1) - position_ref[...]
    q_gain[...] = column(q_gain_ref)
    k_gain[...] = column(k_gain_ref)


def table_scratch():
    return [
        pltpu.VMEM((32, 1024), f32),
        pltpu.VMEM((32, 1024), f32),
        pltpu.VMEM((1, 1024), jnp.int32),
        pltpu.VMEM((64, 1), f32),
        pltpu.VMEM((64, 1), f32),
    ]


def turn(values):
    return values.astype(f32).T.astype(bf16)


def ffn_block(here, low):
    rows = low.rows[here, :]
    gate = dot(rows, low.full[:, 0:1152])
    up = dot(rows, low.full[:, 1152:2304])
    sigmoid = jax.nn.sigmoid(gate)
    silu = gate * sigmoid
    activation = (silu * up).astype(bf16)
    low.activation[here, :] = activation
    hidden = dot(low.grad_rows[here, :], low.full[:, 2304:3456])
    gate_low = (hidden * up * sigmoid * (1.0 + gate * (1.0 - sigmoid))).astype(bf16)
    up_low = (hidden * silu).astype(bf16)
    low.gate_low[here, :] = gate_low
    low.up_low[here, :] = up_low
    low.ffn_part[here, :] = dot_tb(activation, low.full[:, 2304:3456]).astype(bf16)
    low.part[here, :] = (
        dot_tb(gate_low, low.full[:, 0:1152]) + dot_tb(up_low, low.full[:, 1152:2304])
    ).astype(bf16)
    low.rows_t[:, here] = turn(rows)


def front_kernel(
    x_ref, position_ref, gain_ref, wq_ref, wk_ref, wv_ref, wo_ref, q_gain_ref, k_gain_ref, ffn_gain_ref,
    wg_ref, wu_ref, wd_ref, cot_ref,
    attn_full, normed_ref, pre_ref, mixed_ref, lse_ref, q_ref, kt_ref, k_ref, v_ref,
    ffn_grad, middle_grad, out_ref, ffn_gain_part,
    ffn_full, grad_rows, grad_rows_t, rows_ref, rows_t, middle, vt, acc, part, ffn_part,
    activation, gate_low, up_low, *scratch,
):
    me = Place()
    scratch = list(scratch)

    def take(count):
        taken = scratch[:count]
        del scratch[:count]
        return taken

    cos, sin, start, q_gain, k_gain = take(5)
    buffers = take(5)
    scatter = TokenScatter(me, part, *buffers)
    first = TokenScatter(me, part, *buffers)
    last = TokenScatter(me, ffn_part, *take(5))
    attn = WeightGather(me, attn_full, *take(2))
    ffn = WeightGather(me, ffn_full, *take(2))
    tokens = TokenGather(me, normed_ref, *take(2))
    upstream = TokenGather(me, grad_rows, *take(2))
    second = TokenGather(me, rows_ref, *take(2))
    low = Fields(
        cos=cos, sin=sin, q_gain=q_gain, k_gain=k_gain, start=start,
        q=q_ref, kt=kt_ref, k=k_ref, vt=vt, v=v_ref, lse=lse_ref, mixed=mixed_ref,
        rows=rows_ref, rows_t=rows_t, full=ffn_full, grad_rows=grad_rows, part=part, ffn_part=ffn_part,
        activation=activation, gate_low=gate_low, up_low=up_low,
    )
    own_rows = pl.ds(pl.multiple_of(me.d * 32, 32), 32)
    own_tokens = pl.ds(pl.multiple_of(me.t * 256, 256), 256)
    attn_full[own_rows, 0:256] = wq_ref[...]
    attn_full[own_rows, 256:384] = wk_ref[...]
    attn_full[own_rows, 384:512] = wv_ref[...]
    attn_full[own_rows, 512:768] = turn(wo_ref[...])
    values = x_ref[...].astype(f32)
    normed_ref[own_tokens, :] = (values * row_scale(values) * gain_ref[...]).astype(bf16)
    greet(ring_devices(me) + [me.core_device(), me.x_device()])
    attn.begin()
    for chunk in range(4):
        tokens.begin(chunk)
    ffn_full[own_rows, 0:1152] = wg_ref[...]
    ffn_full[own_rows, 1152:2304] = wu_ref[...]
    ffn_full[own_rows, 2304:3456] = turn(wd_ref[...])
    grad_rows[own_tokens, :] = cot_ref[...]
    attn.step1()
    lse_ref[...] = jnp.zeros((8, 1024), f32)
    tables(position_ref, q_gain_ref, k_gain_ref, cos, sin, start, q_gain, k_gain)
    attn.step2()
    attn.step3()
    attn.step4()
    ffn.begin()
    for chunk in range(4):
        tokens.pass_on(chunk)
    tokens.finish()
    attn.finish()
    services = gather_services(ffn)

    def serve(count=1):
        for _ in range(count):
            if services:
                services.pop(0)()

    serve()
    for chunk in range(4):
        upstream.begin(chunk)

    @pl.loop(0, 4)
    def _(block):
        project_block(block, normed_ref, attn_full, pre_ref, low)

    for number in range(4):
        for head in range(2):
            forward_block(low, head, number, acc)
            if number == 1 or number == 3:
                serve()
    for chunk in range(4):
        upstream.pass_on(chunk)

    def output_part(dx, dc):
        here = pl.ds(pl.multiple_of(me.token_block(dx, dc) * 256, 256), 256)
        flat = mixed_ref[:, here].T.astype(bf16)
        part[here, :] = dot_tb(flat, attn_full[:, 512:768]).astype(bf16)

    output_part(1, 1)
    for chunk in range(4):
        scatter.begin_far(chunk)
    output_part(1, 0)
    output_part(0, 1)
    for chunk in range(4):
        scatter.begin_near(chunk)
    output_part(0, 0)
    for chunk in range(4):
        scatter.relay_on(chunk)
    serve(2)
    upstream.finish()
    grad_rows_t[...] = turn(grad_rows[...])
    for chunk in range(4):
        here = pl.ds(chunk * 64, 64)
        values = x_ref[here, :].astype(f32) + scatter.total(chunk)
        middle[here, :] = values
        own = pl.ds(pl.multiple_of(me.t * 256 + chunk * 64, 64), 64)
        rows_ref[own, :] = (values * row_scale(values) * ffn_gain_ref[...]).astype(bf16)
        if chunk == 3:
            scatter.finish()
        second.begin(chunk)
    serve(20)
    ffn.finish()

    passes = [
        remote(piece, piece, second.send, second.recv, 8 + chunk, me.core_device())
        for chunk, piece in enumerate(second.piece(1, 0, chunk) for chunk in range(4))
    ]

    @pl.loop(0, 4)
    def _(turn_number):
        @pl.when(turn_number == 1)
        def _():
            for chunk in range(4):
                second.arrived(second.piece(0, 1, chunk), 4 + chunk)

        @pl.when(turn_number == 2)
        def _():
            for chunk in range(4):
                second.arrived(second.piece(1, 0, chunk), chunk)
                passes[chunk].start()

        @pl.when(turn_number == 3)
        def _():
            for chunk in range(4):
                second.arrived(second.piece(1, 1, chunk), 8 + chunk)

        block = lax.rem(me.xl + lax.div(turn_number, 2), 2) * 2 + lax.rem(me.core + lax.rem(turn_number, 2), 2)
        ffn_block(pl.ds(pl.multiple_of(block * 256, 256), 256), low)

    for copy in second.started + passes:
        copy.wait_send()

    def weight_tile(tile):
        here = pl.ds(tile * 256, 256)
        ffn_grad[here, 0:1152] = dot(rows_t[here, :], gate_low[...]).astype(bf16)
        ffn_grad[here, 1152:2304] = dot(rows_t[here, :], up_low[...]).astype(bf16)
        ffn_grad[here, 2304:3456] = dot(grad_rows_t[here, :], activation[...]).astype(bf16)

    for chunk in range(4):
        first.begin_far(chunk)
    for chunk in range(4):
        first.begin_near(chunk)
    weight_tile(0)
    for chunk in range(4):
        first.relay_on(chunk)
    for chunk in range(4):
        last.begin_far(chunk)
    for chunk in range(4):
        last.begin_near(chunk)
    weight_tile(1)
    for chunk in range(4):
        last.relay_on(chunk)
    weight_tile(2)
    weight_tile(3)
    gain_total = jnp.zeros((1, 1024), f32)
    for chunk in range(4):
        here = pl.ds(chunk * 64, 64)
        grad = first.total(chunk)
        values = middle[here, :]
        inverse = row_scale(values)
        gain_total = gain_total + jnp.sum(grad * values * inverse, axis=0, keepdims=True)
        middle_grad[here, :] = cot_ref[here, :].astype(f32) + norm_back(
            values, inverse, ffn_gain_ref[...], grad
        )
    ffn_gain_part[...] = gain_total
    for chunk in range(4):
        here = pl.ds(chunk * 64, 64)
        out_ref[here, :] = (middle[here, :] + last.total(chunk)).astype(bf16)
    first.finish()
    last.finish()


def scatter_services(scatter):
    steps = []
    for chunk in range(4):
        steps.append(functools.partial(scatter.step1, chunk))
    for chunk in range(4):
        steps.append(functools.partial(scatter.step2, chunk))
    steps.append(scatter.step3)
    steps.append(scatter.step4)
    steps.append(scatter.step5)
    return steps


def back_kernel(
    ffn_grad, middle_grad, ffn_gain_part, x_ref, position_ref, gain_ref, q_gain_ref, k_gain_ref,
    attn_full, normed_ref, pre_ref, mixed_ref, lse_ref, q_ref, kt_ref, k_ref, v_ref,
    input_grad_ref, attn_shard_ref, ffn_shard_ref, gains_ref,
    rows, part, attn_grad, acc, gt, g, inner, qn, dk, dv, dq, turned, flat, gain_rows, *scratch,
):
    me = Place()
    scratch = list(scratch)

    def take(count):
        taken = scratch[:count]
        del scratch[:count]
        return taken

    cos, sin, start, q_gain, k_gain = take(5)
    third = TokenScatter(me, part, *take(5))
    gather = TokenGather(me, rows, *take(2))
    ffn = GradScatter(me, ffn_grad, *take(7))
    attn = GradScatter(me, attn_grad, *take(7))
    gains = GainSum(me, *take(4))
    low = Fields(
        cos=cos, sin=sin, q_gain=q_gain, k_gain=k_gain, start=start,
        q=q_ref, kt=kt_ref, k=k_ref, v=v_ref, lse=lse_ref, mixed=mixed_ref,
        gt=gt, g=g, inner=inner, qn=qn, dk=dk, dv=dv, dq=dq,
    )
    own_tokens = pl.ds(pl.multiple_of(me.t * 256, 256), 256)
    rows[own_tokens, :] = middle_grad[...].astype(bf16)
    greet(gains.row_devices() + gains.plane_devices())
    for chunk in range(4):
        gather.begin(chunk)
    ffn.begin()
    tables(position_ref, q_gain_ref, k_gain_ref, cos, sin, start, q_gain, k_gain)
    services = scatter_services(ffn)

    def serve(count=1):
        for _ in range(count):
            if services:
                services.pop(0)()

    for chunk in range(4):
        gather.pass_on(chunk)
    serve(1)
    gather.finish()

    @pl.loop(0, 4)
    def _(block):
        backward_prepare(block, rows, attn_full, low)

    serve(2)
    for number in range(4):
        for head in range(2):
            backward_block(low, head, number, acc)
            if number >= 1 and head == 1 or number == 3:
                serve()
    q_part = jnp.zeros((64, 1), f32)
    k_part = jnp.zeros((64, 1), f32)
    for block in range(4):
        q_more, k_more = backward_finish(block, low, pre_ref, turned, flat)
        q_part = q_part + q_more
        k_part = k_part + k_more

    def first_part(dx, dc):
        here = pl.ds(pl.multiple_of(me.token_block(dx, dc) * 256, 256), 256)
        part[here, :] = dot_tb(flat[here, :], attn_full[:, 0:512]).astype(bf16)

    first_part(1, 1)
    for chunk in range(4):
        third.begin_far(chunk)
    first_part(1, 0)
    for chunk in range(4):
        third.relay_on(chunk)
    mixed_low = mixed_ref[...].astype(bf16)
    for tile in range(4):
        here = pl.ds(tile * 256, 256)
        attn_grad[here, 0:512] = dot(turned[...], normed_ref[:, here]).T.astype(bf16)
        attn_grad[here, 512:768] = dot(mixed_low, rows[:, here]).T.astype(bf16)
    attn.begin()
    first_part(0, 1)
    for chunk in range(4):
        third.begin_near(chunk)
    first_part(0, 0)
    gain_rows[16:24, :] = jnp.zeros((8, 128), f32)
    gain_rows[16:17, 0:64] = jnp.broadcast_to(q_part, (64, 128)).T[0:1, :]
    gain_rows[17:18, 0:64] = jnp.broadcast_to(k_part, (64, 128)).T[0:1, :]
    serve(20)
    for chunk in range(4):
        attn.step1(chunk)
    gain_total = jnp.zeros((1, 1024), f32)
    for chunk in range(4):
        here = pl.ds(chunk * 64, 64)
        upstream = third.total(chunk)
        values = x_ref[here, :].astype(f32)
        inverse = row_scale(values)
        gain_total = gain_total + jnp.sum(upstream * values * inverse, axis=0, keepdims=True)
        input_grad_ref[here, :] = middle_grad[here, :] + norm_back(
            values, inverse, gain_ref[...], upstream
        )
    for part_number in range(8):
        lanes = slice(128 * part_number, 128 * part_number + 128)
        gain_rows[part_number : part_number + 1, :] = gain_total[:, lanes]
        gain_rows[8 + part_number : 9 + part_number, :] = ffn_gain_part[:, lanes]
    for chunk in range(4):
        attn.step2(chunk)
    attn.step3()
    gains_ref[...] = gains.run(gain_rows[...])
    attn.step4()
    attn.step5()
    ffn_shard_ref[...] = ffn.result()
    attn_shard_ref[...] = attn.result()
    for transfer in (third, ffn, attn):
        transfer.finish()


def unpack_kernel(
    out_ref, input_grad_ref, attn_ref, ffn_ref, gains_ref,
    out, input_grad, attn_gain, wq, wk, wv, wo, q_gain, k_gain, ffn_gain, wg, wu, wd,
):
    out[...] = out_ref[...]
    input_grad[...] = input_grad_ref[...]
    for part in range(8):
        lanes = slice(128 * part, 128 * part + 128)
        attn_gain[:, lanes] = gains_ref[part : part + 1, :]
        ffn_gain[:, lanes] = gains_ref[8 + part : 9 + part, :]
    q_gain[...] = gains_ref[16:17, 0:64]
    k_gain[...] = gains_ref[17:18, 0:64]
    wq[...] = attn_ref[:, 0:256]
    wk[...] = attn_ref[:, 256:384]
    wv[...] = attn_ref[:, 384:512]
    wo[...] = attn_ref[:, 512:768].T
    wg[...] = ffn_ref[:, 0:1152]
    wu[...] = ffn_ref[:, 1152:2304]
    wd[...] = ffn_ref[:, 2304:3456].T


def shape(rows, columns, kind):
    return jax.ShapeDtypeStruct((rows, columns), kind)


def sems(count):
    return [pltpu.SemaphoreType.DMA((count,))] * 2


def body(
    block_input,
    positions,
    attn_gain,
    w_query,
    w_key,
    w_value,
    w_output,
    q_gain,
    k_gain,
    ffn_gain,
    w_gate,
    w_up,
    w_down,
    cotangent,
):
    square = shape(1024, 1024, bf16)
    position_row = positions[None, :]
    (
        attn_full, normed_rows, pre, mixed, lse, q_low, kt_low, k_low, v_low,
        ffn_grad, middle_grad, layer_output, ffn_gain_part,
    ) = call(
        front_kernel,
        [
            shape(1024, 768, bf16),
            square,
            shape(384, 1024, f32),
            shape(256, 1024, f32),
            shape(8, 1024, f32),
            shape(256, 1024, bf16),
            jax.ShapeDtypeStruct((2, 4, 64, 256), bf16),
            jax.ShapeDtypeStruct((2, 1024, 64), bf16),
            jax.ShapeDtypeStruct((2, 1024, 64), bf16),
            shape(1024, 3456, bf16),
            shape(256, 1024, f32),
            shape(256, 1024, bf16),
            shape(1, 1024, f32),
        ],
        [
            pltpu.VMEM((1024, 3456), bf16),
            pltpu.VMEM((1024, 1024), bf16),
            pltpu.VMEM((1024, 1024), bf16),
            pltpu.VMEM((1024, 1024), bf16),
            pltpu.VMEM((1024, 1024), bf16),
            pltpu.VMEM((256, 1024), f32),
            pltpu.VMEM((2, 4, 80, 256), bf16),
            pltpu.VMEM((80, 512), f32),
            pltpu.VMEM((1024, 1024), bf16),
            pltpu.VMEM((1024, 1024), bf16),
            pltpu.VMEM((1024, 1152), bf16),
            pltpu.VMEM((1024, 1152), bf16),
            pltpu.VMEM((1024, 1152), bf16),
        ]
        + table_scratch()
        + scatter_scratch() * 2
        + sems(41) * 2
        + sems(12) * 3,
        0,
        (
            block_input, position_row, attn_gain[None, :], w_query, w_key, w_value, w_output,
            q_gain[None, :], k_gain[None, :], ffn_gain[None, :], w_gate, w_up, w_down, cotangent,
        ),
    )
    input_grad, attn_out, ffn_out, gains = call(
        back_kernel,
        [
            shape(256, 1024, f32),
            shape(32, 768, f32),
            shape(32, 3456, f32),
            shape(24, 128, f32),
        ],
        [
            pltpu.VMEM((1024, 1024), bf16),
            pltpu.VMEM((1024, 1024), bf16),
            pltpu.VMEM((1024, 768), bf16),
            pltpu.VMEM((80, 512), f32),
            pltpu.VMEM((256, 1024), bf16),
            pltpu.VMEM((4, 1024, 64), bf16),
            pltpu.VMEM((8, 1024), f32),
            pltpu.VMEM((4, 1024, 64), bf16),
            pltpu.VMEM((2, 1024, 64), f32),
            pltpu.VMEM((2, 1024, 64), f32),
            pltpu.VMEM((256, 1024), f32),
            pltpu.VMEM((512, 1024), bf16),
            pltpu.VMEM((1024, 512), bf16),
            pltpu.VMEM((24, 128), f32),
        ]
        + table_scratch()
        + scatter_scratch()
        + sems(12)
        + grad_scratch(3456)
        + grad_scratch(768)
        + gain_scratch(),
        1,
        (
            ffn_grad, middle_grad, ffn_gain_part, block_input, position_row, attn_gain[None, :],
            q_gain[None, :], k_gain[None, :],
            attn_full, normed_rows, pre, mixed, lse, q_low, kt_low, k_low, v_low,
        ),
    )
    outs = pl.pallas_call(
        unpack_kernel,
        out_shape=[
            shape(256, 1024, bf16),
            shape(256, 1024, f32),
            shape(1, 1024, f32),
            shape(32, 256, f32),
            shape(32, 128, f32),
            shape(32, 128, f32),
            shape(256, 32, f32),
            shape(1, 64, f32),
            shape(1, 64, f32),
            shape(1, 1024, f32),
            shape(32, 1152, f32),
            shape(32, 1152, f32),
            shape(1152, 32, f32),
        ],
        in_specs=[VMEM_SPEC] * 5,
        out_specs=[VMEM_SPEC] * 13,
        compiler_params=pltpu.CompilerParams(vmem_limit_bytes=VMEM_LIMIT),
    )(layer_output, input_grad, attn_out, ffn_out, gains)
    return tuple(out[0] if out.shape[0] == 1 else out for out in outs)


def solution(mesh):
    placed = (
        P(("dp", "tensor"), None),
        P("dp"),
        P(),
        P("dp", "tensor"),
        P("dp", "tensor"),
        P("dp", "tensor"),
        P("tensor", "dp"),
        P(),
        P(),
        P(),
        P("dp", "tensor"),
        P("dp", "tensor"),
        P("tensor", "dp"),
        P(("dp", "tensor"), None),
    )
    return jax.shard_map(
        body,
        mesh=mesh,
        in_specs=placed,
        out_specs=(
            P(("dp", "tensor"), None),
            P(("dp", "tensor"), None),
            P(),
            P("dp", "tensor"),
            P("dp", "tensor"),
            P("dp", "tensor"),
            P("tensor", "dp"),
            P(),
            P(),
            P(),
            P("dp", "tensor"),
            P("dp", "tensor"),
            P("tensor", "dp"),
        ),
        check_vma=False,
    )
```

profile of v0, /device:TPU:0, one launch (start us, length us, event | category | flops | bytes accessed | tf_op | source)
XLA Modules:
  0.0 213.4 jit_solution(15672092359112540904)
XLA Ops:
  0.6 1.5 copy.27.wo_ref
  2.1 1.8 copy.28.wd_ref
  3.9 119.5 %shard_map.237 = (bf16[1024,768]{1,0:T(8,128)(2,1)}, bf16[1024,1024]{1,0:T(8,128)(2,1)}, f32[384,1024]{1,0:T(8,128)}, f32[256,1024]{1,0:T(8,128)}, f32[8,1024]{1...) custom-call(bf16[256,1024]{1,0:T(8,128)(2,1)} %x_ref.3, ...), custom_call_target="tpu_custom_call" | custom-call | tf_op jit(solution)/shard_map/pallas_call | solution.py:419
  123.3 83.2 %shard_map.238 = (f32[256,1024]{1,0:T(8,128)}, f32[32,768]{1,0:T(8,128)}, f32[32,3456]{1,0:T(8,128)}, f32[24,128]{1,0:T(8,128)}) custom-call(bf16[1024,3456]{1,0:T(8,128)(2,1)} %get-tuple-element.44.ffn_grad, f32[256,1024]{1,0:T(8,128)} %get-tuple-element.45.middle_grad, f32[1,1024]{1,0:T(1,128)} %get-tuple-element.46.ffn_gain_part, ...), custom_call_target="tpu_custom_call" | custom-call | tf_op jit(solution)/shard_map/pallas_call | solution.py:419
  206.6 3.3 %shard_map.239 = (bf16[256,1024]{1,0:T(8,128)(2,1)}, f32[256,1024]{1,0:T(8,128)}, f32[1,1024]{1,0:T(1,128)}, f32[32,256]{1,0:T(8,128)}, f32[32,128]{1,0:T(8,128)...) custom-call(bf16[256,1024]{1,0:T(8,128)(2,1)} %get-tuple-element.43., ...), custom_call_target="tpu_custom_call" | custom-call | tf_op jit(solution)/shard_map/pallas_call | solution.py:1162
  209.8 1.6 copy.29
  211.4 1.9 copy.30
where the time goes:
time: 214 us; the launch traced here: 213 us
  Pallas kernels  206 us (96%)
  local copies, waits for them, and re-layouts  6.75 us (3%)
    pallas_call x2, Pallas kernels, call(): pl.pallas_call(kernel, out_shape=outs, in_specs=[VMEM_SPEC] * len(args),...  203 us
    unnamed x4, local copies, waits for them, and re-layouts  6.75 us

commit v1 on v0

--- a/solution.py
+++ b/solution.py
@@ -14,7 +14,7 @@
 bf16 = jnp.bfloat16
 MESH = pl.DeviceIdType.MESH
 VMEM_SPEC = pl.BlockSpec(memory_space=pltpu.VMEM)
-VMEM_LIMIT = 60 * 1024 * 1024
+VMEM_LIMIT = 62 * 1024 * 1024
 
 
 class Place:
@@ -267,10 +267,10 @@
 class GradScatter:
     COUNT = 61
 
-    def __init__(self, me, part, recv_half, recv_full, out_half, sums, last, send, recv):
+    def __init__(self, me, part, recv_half, recv_full, sums, last, send, recv):
         self.me, self.part = me, part
         self.recv_half, self.recv_full = recv_half, recv_full
-        self.out_half, self.sums, self.last = out_half, sums, last
+        self.sums, self.last = sums, last
         self.send, self.recv = send, recv
         self.started = []
 
@@ -332,9 +332,9 @@
         ref, _, halves = self.source(kind, level, chunk, step)
         self.arrived(self.recv_half.at[slot, side], slot * 6 + side)
         total = ref[halves[side], :].astype(f32) + self.recv_half[slot, side].astype(f32)
-        self.out_half[slot, side] = total.astype(bf16)
+        ref[halves[side], :] = total.astype(bf16)
         self.push(
-            self.out_half.at[slot, side],
+            ref.at[halves[side]],
             self.recv_full.at[slot, side, pl.ds(16 * side, 16)],
             slot * 6 + 2 + side,
             self.along(kind, level, step),
@@ -397,7 +397,6 @@
     return [
         pltpu.VMEM((10, 2, 16, width), bf16),
         pltpu.VMEM((10, 2, 32, width), bf16),
-        pltpu.VMEM((10, 2, 16, width), bf16),
         pltpu.VMEM((256, width), bf16),
         pltpu.VMEM((2, 32, width), bf16),
         pltpu.SemaphoreType.DMA((61,)),
@@ -706,31 +705,57 @@
 
 def ffn_block(here, low):
     rows = low.rows[here, :]
-    gate = dot(rows, low.full[:, 0:1152])
-    up = dot(rows, low.full[:, 1152:2304])
-    sigmoid = jax.nn.sigmoid(gate)
-    silu = gate * sigmoid
-    activation = (silu * up).astype(bf16)
-    low.activation[here, :] = activation
-    hidden = dot(low.grad_rows[here, :], low.full[:, 2304:3456])
-    gate_low = (hidden * up * sigmoid * (1.0 + gate * (1.0 - sigmoid))).astype(bf16)
-    up_low = (hidden * silu).astype(bf16)
-    low.gate_low[here, :] = gate_low
-    low.up_low[here, :] = up_low
-    low.ffn_part[here, :] = dot_tb(activation, low.full[:, 2304:3456]).astype(bf16)
+    grads = low.grad_rows[here, :]
+    for first, count in ((0, 512), (512, 640)):
+        columns = pl.ds(first, count)
+        gate = dot(rows, low.full[:, pl.ds(first, count)])
+        up = dot(rows, low.full[:, pl.ds(1152 + first, count)])
+        hidden = dot(grads, low.full[:, pl.ds(2304 + first, count)])
+        sigmoid = jax.nn.sigmoid(gate)
+        silu = gate * sigmoid
+        low.activation[here, columns] = (silu * up).astype(bf16)
+        low.gate_low[here, columns] = (hidden * up * sigmoid * (1.0 + gate * (1.0 - sigmoid))).astype(bf16)
+        low.up_low[here, columns] = (hidden * silu).astype(bf16)
+    low.ffn_part[here, :] = dot_tb(low.activation[here, :], low.full[:, 2304:3456]).astype(bf16)
     low.part[here, :] = (
-        dot_tb(gate_low, low.full[:, 0:1152]) + dot_tb(up_low, low.full[:, 1152:2304])
+        dot_tb(low.gate_low[here, :], low.full[:, 0:1152]) + dot_tb(low.up_low[here, :], low.full[:, 1152:2304])
     ).astype(bf16)
-    low.rows_t[:, here] = turn(rows)
-
-
-def front_kernel(
+
+
+def scatter_services(scatter):
+    steps = []
+    for chunk in range(4):
+        steps.append(functools.partial(scatter.step1, chunk))
+    for chunk in range(4):
+        steps.append(functools.partial(scatter.step2, chunk))
+    steps.append(scatter.step3)
+    steps.append(scatter.step4)
+    steps.append(scatter.step5)
+    return steps
+
+
+class Heads:
+    def __init__(self, ref, first):
+        self.ref, self.first = ref, first
+
+    def lanes(self, head):
+        return pl.ds((self.first + head) * 128, 64)
+
+    def __getitem__(self, index):
+        return self.ref[index[1], self.lanes(index[0])]
+
+    def __setitem__(self, index, value):
+        self.ref[index[1], self.lanes(index[0])] = value
+
+
+def block_kernel(
     x_ref, position_ref, gain_ref, wq_ref, wk_ref, wv_ref, wo_ref, q_gain_ref, k_gain_ref, ffn_gain_ref,
     wg_ref, wu_ref, wd_ref, cot_ref,
-    attn_full, normed_ref, pre_ref, mixed_ref, lse_ref, q_ref, kt_ref, k_ref, v_ref,
-    ffn_grad, middle_grad, out_ref, ffn_gain_part,
-    ffn_full, grad_rows, grad_rows_t, rows_ref, rows_t, middle, vt, acc, part, ffn_part,
-    activation, gate_low, up_low, *scratch,
+    out_ref, input_grad_ref, attn_shard_ref, ffn_shard_ref, gains_ref,
+    attn_full, ffn_full, normed_ref, grad_rows, grad_rows_t, rows_ref, back_rows, middle, part, ffn_part,
+    activation, gate_low, up_low,
+    pre_ref, mixed_ref, lse_ref, q_ref, kt_ref, k_ref, vt, v_ref, acc, inner, dk, dv, dq, gain_rows,
+    *scratch,
 ):
     me = Place()
     scratch = list(scratch)
@@ -744,33 +769,44 @@
     buffers = take(5)
     scatter = TokenScatter(me, part, *buffers)
     first = TokenScatter(me, part, *buffers)
+    third = TokenScatter(me, part, *buffers)
     last = TokenScatter(me, ffn_part, *take(5))
     attn = WeightGather(me, attn_full, *take(2))
     ffn = WeightGather(me, ffn_full, *take(2))
     tokens = TokenGather(me, normed_ref, *take(2))
     upstream = TokenGather(me, grad_rows, *take(2))
     second = TokenGather(me, rows_ref, *take(2))
+    back = TokenGather(me, back_rows, *take(2))
+    attn_grad = grad_rows_t.at[:, pl.ds(0, 768)]
+    ffn_grad = GradScatter(me, ffn_full, *take(6))
+    weight_grad = GradScatter(me, attn_grad, *take(6))
+    gains = GainSum(me, *take(4))
+    middle_grad = input_grad_ref
+    turned = gate_low.at[pl.ds(0, 512), pl.ds(0, 1024)]
+    flat = up_low.at[:, pl.ds(0, 512)]
+    gt = gate_low.at[pl.ds(512, 256), pl.ds(0, 1024)]
     low = Fields(
         cos=cos, sin=sin, q_gain=q_gain, k_gain=k_gain, start=start,
         q=q_ref, kt=kt_ref, k=k_ref, vt=vt, v=v_ref, lse=lse_ref, mixed=mixed_ref,
-        rows=rows_ref, rows_t=rows_t, full=ffn_full, grad_rows=grad_rows, part=part, ffn_part=ffn_part,
+        rows=rows_ref, full=ffn_full, grad_rows=grad_rows, part=part, ffn_part=ffn_part,
         activation=activation, gate_low=gate_low, up_low=up_low,
+        gt=gt, g=Heads(activation, 0), inner=inner, qn=Heads(activation, 4), dk=dk, dv=dv, dq=dq,
     )
     own_rows = pl.ds(pl.multiple_of(me.d * 32, 32), 32)
     own_tokens = pl.ds(pl.multiple_of(me.t * 256, 256), 256)
     attn_full[own_rows, 0:256] = wq_ref[...]
     attn_full[own_rows, 256:384] = wk_ref[...]
     attn_full[own_rows, 384:512] = wv_ref[...]
-    attn_full[own_rows, 512:768] = turn(wo_ref[...])
+    attn_full[own_rows, 512:768] = wo_ref[...]
     values = x_ref[...].astype(f32)
     normed_ref[own_tokens, :] = (values * row_scale(values) * gain_ref[...]).astype(bf16)
-    greet(ring_devices(me) + [me.core_device(), me.x_device()])
+    greet(gains.row_devices() + gains.plane_devices())
     attn.begin()
     for chunk in range(4):
         tokens.begin(chunk)
     ffn_full[own_rows, 0:1152] = wg_ref[...]
     ffn_full[own_rows, 1152:2304] = wu_ref[...]
-    ffn_full[own_rows, 2304:3456] = turn(wd_ref[...])
+    ffn_full[own_rows, 2304:3456] = wd_ref[...]
     grad_rows[own_tokens, :] = cot_ref[...]
     attn.step1()
     lse_ref[...] = jnp.zeros((8, 1024), f32)
@@ -823,7 +859,12 @@
         scatter.relay_on(chunk)
     serve(2)
     upstream.finish()
-    grad_rows_t[...] = turn(grad_rows[...])
+
+    @pl.loop(0, 4)
+    def _(block):
+        here = pl.ds(pl.multiple_of(block * 256, 256), 256)
+        grad_rows_t[:, here] = turn(grad_rows[here, :])
+
     for chunk in range(4):
         here = pl.ds(chunk * 64, 64)
         values = x_ref[here, :].astype(f32) + scatter.total(chunk)
@@ -865,112 +906,68 @@
     for copy in second.started + passes:
         copy.wait_send()
 
+    for chunk in range(4):
+        first.begin_far(chunk)
+    for chunk in range(4):
+        first.begin_near(chunk)
+
     def weight_tile(tile):
-        here = pl.ds(tile * 256, 256)
-        ffn_grad[here, 0:1152] = dot(rows_t[here, :], gate_low[...]).astype(bf16)
-        ffn_grad[here, 1152:2304] = dot(rows_t[here, :], up_low[...]).astype(bf16)
-        ffn_grad[here, 2304:3456] = dot(grad_rows_t[here, :], activation[...]).astype(bf16)
-
-    for chunk in range(4):
-        first.begin_far(chunk)
-    for chunk in range(4):
-        first.begin_near(chunk)
-    weight_tile(0)
+        here = pl.ds(pl.multiple_of(tile * 256, 256), 256)
+        rows_t = turn(rows_ref[:, here])
+        ffn_full[here, 0:1152] = dot(rows_t, gate_low[...]).astype(bf16)
+        ffn_full[here, 1152:2304] = dot(rows_t, up_low[...]).astype(bf16)
+        ffn_full[here, 2304:3456] = dot(grad_rows_t[here, :], activation[...]).astype(bf16)
+
+    pl.loop(0, 1)(weight_tile)
     for chunk in range(4):
         first.relay_on(chunk)
-    for chunk in range(4):
-        last.begin_far(chunk)
-    for chunk in range(4):
-        last.begin_near(chunk)
-    weight_tile(1)
-    for chunk in range(4):
-        last.relay_on(chunk)
-    weight_tile(2)
-    weight_tile(3)
-    gain_total = jnp.zeros((1, 1024), f32)
+    pl.loop(1, 4)(weight_tile)
+    ffn_grad.begin()
+    ffn_gain_total = jnp.zeros((1, 1024), f32)
     for chunk in range(4):
         here = pl.ds(chunk * 64, 64)
         grad = first.total(chunk)
         values = middle[here, :]
         inverse = row_scale(values)
-        gain_total = gain_total + jnp.sum(grad * values * inverse, axis=0, keepdims=True)
-        middle_grad[here, :] = cot_ref[here, :].astype(f32) + norm_back(
-            values, inverse, ffn_gain_ref[...], grad
-        )
-    ffn_gain_part[...] = gain_total
-    for chunk in range(4):
-        here = pl.ds(chunk * 64, 64)
-        out_ref[here, :] = (middle[here, :] + last.total(chunk)).astype(bf16)
-    first.finish()
-    last.finish()
-
-
-def scatter_services(scatter):
-    steps = []
-    for chunk in range(4):
-        steps.append(functools.partial(scatter.step1, chunk))
-    for chunk in range(4):
-        steps.append(functools.partial(scatter.step2, chunk))
-    steps.append(scatter.step3)
-    steps.append(scatter.step4)
-    steps.append(scatter.step5)
-    return steps
-
-
-def back_kernel(
-    ffn_grad, middle_grad, ffn_gain_part, x_ref, position_ref, gain_ref, q_gain_ref, k_gain_ref,
-    attn_full, normed_ref, pre_ref, mixed_ref, lse_ref, q_ref, kt_ref, k_ref, v_ref,
-    input_grad_ref, attn_shard_ref, ffn_shard_ref, gains_ref,
-    rows, part, attn_grad, acc, gt, g, inner, qn, dk, dv, dq, turned, flat, gain_rows, *scratch,
-):
-    me = Place()
-    scratch = list(scratch)
-
-    def take(count):
-        taken = scratch[:count]
-        del scratch[:count]
-        return taken
-
-    cos, sin, start, q_gain, k_gain = take(5)
-    third = TokenScatter(me, part, *take(5))
-    gather = TokenGather(me, rows, *take(2))
-    ffn = GradScatter(me, ffn_grad, *take(7))
-    attn = GradScatter(me, attn_grad, *take(7))
-    gains = GainSum(me, *take(4))
-    low = Fields(
-        cos=cos, sin=sin, q_gain=q_gain, k_gain=k_gain, start=start,
-        q=q_ref, kt=kt_ref, k=k_ref, v=v_ref, lse=lse_ref, mixed=mixed_ref,
-        gt=gt, g=g, inner=inner, qn=qn, dk=dk, dv=dv, dq=dq,
-    )
-    own_tokens = pl.ds(pl.multiple_of(me.t * 256, 256), 256)
-    rows[own_tokens, :] = middle_grad[...].astype(bf16)
-    greet(gains.row_devices() + gains.plane_devices())
-    for chunk in range(4):
-        gather.begin(chunk)
-    ffn.begin()
-    tables(position_ref, q_gain_ref, k_gain_ref, cos, sin, start, q_gain, k_gain)
-    services = scatter_services(ffn)
-
-    def serve(count=1):
-        for _ in range(count):
-            if services:
-                services.pop(0)()
-
-    for chunk in range(4):
-        gather.pass_on(chunk)
+        ffn_gain_total = ffn_gain_total + jnp.sum(grad * values * inverse, axis=0, keepdims=True)
+        total = cot_ref[here, :].astype(f32) + norm_back(values, inverse, ffn_gain_ref[...], grad)
+        middle_grad[here, :] = total
+        own = pl.ds(pl.multiple_of(me.t * 256 + chunk * 64, 64), 64)
+        back_rows[own, :] = total.astype(bf16)
+        if chunk == 3:
+            first.finish()
+        back.begin(chunk)
+    for chunk in range(4):
+        last.begin_far(chunk)
+    for chunk in range(4):
+        last.begin_near(chunk)
+    services.extend(scatter_services(ffn_grad))
+    serve(3)
+    for chunk in range(4):
+        back.pass_on(chunk)
+    for chunk in range(4):
+        last.relay_on(chunk)
     serve(1)
-    gather.finish()
+    back.finish()
 
     @pl.loop(0, 4)
     def _(block):
-        backward_prepare(block, rows, attn_full, low)
-
-    serve(2)
+        backward_prepare(block, back_rows, attn_full, low)
+
+
+    @pl.loop(0, 4)
+    def _(tile):
+        here = pl.ds(pl.multiple_of(tile * 256, 256), 256)
+        attn_grad[here, 512:768] = dot(mixed_ref[...].astype(bf16), back_rows[:, here]).T.astype(bf16)
+
     for number in range(4):
         for head in range(2):
             backward_block(low, head, number, acc)
-            if number >= 1 and head == 1 or number == 3:
+            if number == 3:
                 serve()
+    for chunk in range(4):
+        here = pl.ds(chunk * 64, 64)
+        out_ref[here, :] = (middle[here, :] + last.total(chunk)).astype(bf16)
     q_part = jnp.zeros((64, 1), f32)
     k_part = jnp.zeros((64, 1), f32)
     for block in range(4):
@@ -978,6 +975,8 @@
         q_part = q_part + q_more
         k_part = k_part + k_more
 
+    serve(2)
+
     def first_part(dx, dc):
         here = pl.ds(pl.multiple_of(me.token_block(dx, dc) * 256, 256), 256)
         part[here, :] = dot_tb(flat[here, :], attn_full[:, 0:512]).astype(bf16)
@@ -988,12 +987,13 @@
     first_part(1, 0)
     for chunk in range(4):
         third.relay_on(chunk)
-    mixed_low = mixed_ref[...].astype(bf16)
-    for tile in range(4):
-        here = pl.ds(tile * 256, 256)
+
+    @pl.loop(0, 4)
+    def _(tile):
+        here = pl.ds(pl.multiple_of(tile * 256, 256), 256)
         attn_grad[here, 0:512] = dot(turned[...], normed_ref[:, here]).T.astype(bf16)
-        attn_grad[here, 512:768] = dot(mixed_low, rows[:, here]).T.astype(bf16)
-    attn.begin()
+
+    weight_grad.begin()
     first_part(0, 1)
     for chunk in range(4):
         third.begin_near(chunk)
@@ -1003,7 +1003,7 @@
     gain_rows[17:18, 0:64] = jnp.broadcast_to(k_part, (64, 128)).T[0:1, :]
     serve(20)
     for chunk in range(4):
-        attn.step1(chunk)
+        weight_grad.step1(chunk)
     gain_total = jnp.zeros((1, 1024), f32)
     for chunk in range(4):
         here = pl.ds(chunk * 64, 64)
@@ -1017,16 +1017,16 @@
     for part_number in range(8):
         lanes = slice(128 * part_number, 128 * part_number + 128)
         gain_rows[part_number : part_number + 1, :] = gain_total[:, lanes]
-        gain_rows[8 + part_number : 9 + part_number, :] = ffn_gain_part[:, lanes]
-    for chunk in range(4):
-        attn.step2(chunk)
-    attn.step3()
+        gain_rows[8 + part_number : 9 + part_number, :] = ffn_gain_total[:, lanes]
+    for chunk in range(4):
+        weight_grad.step2(chunk)
+    weight_grad.step3()
     gains_ref[...] = gains.run(gain_rows[...])
-    attn.step4()
-    attn.step5()
-    ffn_shard_ref[...] = ffn.result()
-    attn_shard_ref[...] = attn.result()
-    for transfer in (third, ffn, attn):
+    weight_grad.step4()
+    weight_grad.step5()
+    ffn_shard_ref[...] = ffn_grad.result()
+    attn_shard_ref[...] = weight_grad.result()
+    for transfer in (third, last, ffn_grad, weight_grad):
         transfer.finish()
 
 
@@ -1045,10 +1045,10 @@
     wq[...] = attn_ref[:, 0:256]
     wk[...] = attn_ref[:, 256:384]
     wv[...] = attn_ref[:, 384:512]
-    wo[...] = attn_ref[:, 512:768].T
+    wo[...] = attn_ref[:, 512:768]
     wg[...] = ffn_ref[:, 0:1152]
     wu[...] = ffn_ref[:, 1152:2304]
-    wd[...] = ffn_ref[:, 2304:3456].T
+    wd[...] = ffn_ref[:, 2304:3456]
 
 
 def shape(rows, columns, kind):
@@ -1075,88 +1075,57 @@
     w_down,
     cotangent,
 ):
-    square = shape(1024, 1024, bf16)
-    position_row = positions[None, :]
-    (
-        attn_full, normed_rows, pre, mixed, lse, q_low, kt_low, k_low, v_low,
-        ffn_grad, middle_grad, layer_output, ffn_gain_part,
-    ) = call(
-        front_kernel,
+    square = pltpu.VMEM((1024, 1024), bf16)
+    hidden = pltpu.VMEM((1024, 1152), bf16)
+    layer_output, input_grad, attn_out, ffn_out, gains = call(
+        block_kernel,
         [
-            shape(1024, 768, bf16),
-            square,
-            shape(384, 1024, f32),
-            shape(256, 1024, f32),
-            shape(8, 1024, f32),
             shape(256, 1024, bf16),
-            jax.ShapeDtypeStruct((2, 4, 64, 256), bf16),
-            jax.ShapeDtypeStruct((2, 1024, 64), bf16),
-            jax.ShapeDtypeStruct((2, 1024, 64), bf16),
-            shape(1024, 3456, bf16),
-            shape(256, 1024, f32),
-            shape(256, 1024, bf16),
-            shape(1, 1024, f32),
-        ],
-        [
-            pltpu.VMEM((1024, 3456), bf16),
-            pltpu.VMEM((1024, 1024), bf16),
-            pltpu.VMEM((1024, 1024), bf16),
-            pltpu.VMEM((1024, 1024), bf16),
-            pltpu.VMEM((1024, 1024), bf16),
-            pltpu.VMEM((256, 1024), f32),
-            pltpu.VMEM((2, 4, 80, 256), bf16),
-            pltpu.VMEM((80, 512), f32),
-            pltpu.VMEM((1024, 1024), bf16),
-            pltpu.VMEM((1024, 1024), bf16),
-            pltpu.VMEM((1024, 1152), bf16),
-            pltpu.VMEM((1024, 1152), bf16),
-            pltpu.VMEM((1024, 1152), bf16),
-        ]
-        + table_scratch()
-        + scatter_scratch() * 2
-        + sems(41) * 2
-        + sems(12) * 3,
-        0,
-        (
-            block_input, position_row, attn_gain[None, :], w_query, w_key, w_value, w_output,
-            q_gain[None, :], k_gain[None, :], ffn_gain[None, :], w_gate, w_up, w_down, cotangent,
-        ),
-    )
-    input_grad, attn_out, ffn_out, gains = call(
-        back_kernel,
-        [
             shape(256, 1024, f32),
             shape(32, 768, f32),
             shape(32, 3456, f32),
             shape(24, 128, f32),
         ],
         [
-            pltpu.VMEM((1024, 1024), bf16),
-            pltpu.VMEM((1024, 1024), bf16),
             pltpu.VMEM((1024, 768), bf16),
+            pltpu.VMEM((1024, 3456), bf16),
+            square,
+            square,
+            square,
+            square,
+            square,
+            pltpu.VMEM((256, 1024), f32),
+            square,
+            square,
+            hidden,
+            hidden,
+            hidden,
+            pltpu.VMEM((384, 1024), f32),
+            pltpu.VMEM((256, 1024), f32),
+            pltpu.VMEM((8, 1024), f32),
+            pltpu.VMEM((256, 1024), bf16),
+            pltpu.VMEM((2, 4, 64, 256), bf16),
+            pltpu.VMEM((2, 1024, 64), bf16),
+            pltpu.VMEM((2, 4, 80, 256), bf16),
+            pltpu.VMEM((2, 1024, 64), bf16),
             pltpu.VMEM((80, 512), f32),
-            pltpu.VMEM((256, 1024), bf16),
-            pltpu.VMEM((4, 1024, 64), bf16),
             pltpu.VMEM((8, 1024), f32),
-            pltpu.VMEM((4, 1024, 64), bf16),
             pltpu.VMEM((2, 1024, 64), f32),
             pltpu.VMEM((2, 1024, 64), f32),
             pltpu.VMEM((256, 1024), f32),
-            pltpu.VMEM((512, 1024), bf16),
-            pltpu.VMEM((1024, 512), bf16),
             pltpu.VMEM((24, 128), f32),
         ]
         + table_scratch()
-        + scatter_scratch()
-        + sems(12)
+        + scatter_scratch() * 2
+        + sems(41) * 2
+        + sems(12) * 4
         + grad_scratch(3456)
         + grad_scratch(768)
         + gain_scratch(),
-        1,
+        0,
         (
-            ffn_grad, middle_grad, ffn_gain_part, block_input, position_row, attn_gain[None, :],
-            q_gain[None, :], k_gain[None, :],
-            attn_full, normed_rows, pre, mixed, lse, q_low, kt_low, k_low, v_low,
+            block_input, positions[None, :], attn_gain[None, :], w_query, w_key, w_value, w_output.T,
+            q_gain[None, :], k_gain[None, :], ffn_gain[None, :], w_gate, w_up, w_down.T, cotangent,
         ),
     )
     outs = pl.pallas_call(
@@ -1168,19 +1137,20 @@
             shape(32, 256, f32),
             shape(32, 128, f32),
             shape(32, 128, f32),
-            shape(256, 32, f32),
+            shape(32, 256, f32),
             shape(1, 64, f32),
             shape(1, 64, f32),
             shape(1, 1024, f32),
             shape(32, 1152, f32),
             shape(32, 1152, f32),
-            shape(1152, 32, f32),
+            shape(32, 1152, f32),
         ],
         in_specs=[VMEM_SPEC] * 5,
         out_specs=[VMEM_SPEC] * 13,
         compiler_params=pltpu.CompilerParams(vmem_limit_bytes=VMEM_LIMIT),
     )(layer_output, input_grad, attn_out, ffn_out, gains)
-    return tuple(out[0] if out.shape[0] == 1 else out for out in outs)
+    outs = [out[0] if out.shape[0] == 1 else out for out in outs]
+    return (*outs[:6], outs[6].T, *outs[7:12], outs[12].T)
 
 
 def solution(mesh):

time: 214 us -> 177 us (0.83)
  Pallas kernels: 206 us -> 176 us
  local copies, waits for them, and re-layouts: 6.75 us -> 0 us
    pallas_call x2 -> x1, Pallas kernels: 203 us -> 173 us  [call(): pl.pallas_call(kernel, out_shape=outs, in_specs=[VMEM_SPEC] * len(args),...]
    unnamed x4 -> x0, local copies, waits for them, and re-layouts: 6.75 us -> none
where the time goes in v1:
time: 177 us
  Pallas kernels  176 us (99%)
    pallas_call x1, Pallas kernels, call(): pl.pallas_call(kernel, out_shape=outs, in_specs=[VMEM_SPEC] * len(args),...  173 us

profile of v1, /device:TPU:0, one launch (start us, length us, event | category | flops | bytes accessed | tf_op | source)
XLA Modules:
  0.0 177.2 jit_solution(7019378680212774807)
XLA Ops:
  0.7 173.5 %shard_map.237 = (bf16[256,1024]{1,0:T(8,128)(2,1)}, f32[256,1024]{1,0:T(8,128)}, f32[32,768]{1,0:T(8,128)}, f32[32,3456]{1,0:T(8,128)}, f32[24,128]{1,0:T(8,128)}) custom-call(bf16[256,1024]{1,0:T(8,128)(2,1)} %x_ref.1, s32[1,1024]{1,0:T(1,128)} %bitcast.15, f32[1,1024]{1,0:T(1,128)} %bitcast.16, bf16[32,256]{1,0:T(8,128)(2,1)} %wq_ref.1, ...), custom_call_target="tpu_custom_call" | custom-call | tf_op jit(solution)/shard_map/pallas_call | solution.py:418
  174.1 2.9 %shard_map.238 = (bf16[256,1024]{1,0:T(8,128)(2,1)}, f32[256,1024]{1,0:T(8,128)}, f32[1,1024]{1,0:T(1,128)}, f32[32,256]{1,0:T(8,128)}, f32[32,128]{1,0:T(8,128)...) custom-call(bf16[256,1024]{1,0:T(8,128)(2,1)} %get-tuple-element.31., ...), custom_call_target="tpu_custom_call" | custom-call | tf_op jit(solution)/shard_map/pallas_call | solution.py:1131

commit v2 on v1

--- a/solution.py
+++ b/solution.py
@@ -85,8 +85,8 @@
 class WeightGather:
     COUNT = 41
 
-    def __init__(self, me, full, send, recv):
-        self.me, self.full, self.send, self.recv = me, full, send, recv
+    def __init__(self, me, full, direct, send, recv):
+        self.me, self.full, self.direct, self.send, self.recv = me, full, direct, send, recv
         self.started = []
 
     def block(self, kind, first, second, part=None):
@@ -117,6 +117,8 @@
         ref = self.block(kind, first, 0)
         self.push(ref, base, self.along(kind, level, 1))
         self.push(ref, base + 1, self.along(kind, level, -1))
+        if level == 0 and self.direct:
+            self.push(ref, base + 2, self.along(kind, level, 2))
 
     def pass_on(self, kind, level, chunk, side):
         first = (0, -1, 1, 2)[chunk] if level == 1 else 0
@@ -133,8 +135,11 @@
         for side in range(2):
             self.arrived(self.block(kind, *where, part=side), base + 2 + side)
 
+    def exchange(self):
+        self.push(self.block(0, 0, 0), 0, self.me.dp_device(dh=1))
+
     def begin(self):
-        self.push(self.block(0, 0, 0), 0, self.me.dp_device(dh=1))
+        self.exchange()
         self.spread(0, 0, 0)
         self.spread(0, 1, 0)
 
@@ -143,16 +148,23 @@
         self.spread(1, 0, 0)
         self.spread(1, 1, 0)
 
+    def hand_on(self, kind, number):
+        if self.direct:
+            self.arrived(self.block(kind, (-1, 1, 2)[number], 0), self.base(kind, 0, 0) + number)
+        elif number < 2:
+            self.pass_on(kind, 0, 0, number)
+        else:
+            self.last(kind, 0, 0)
+        self.spread(kind, 1, 1 + number)
+
     def step2(self):
         for kind in range(2):
-            for side in range(2):
-                self.pass_on(kind, 0, 0, side)
-                self.spread(kind, 1, 1 + side)
+            for number in range(2):
+                self.hand_on(kind, number)
 
     def step3(self):
         for kind in range(2):
-            self.last(kind, 0, 0)
-            self.spread(kind, 1, 3)
+            self.hand_on(kind, 2)
 
     def step4(self):
         for chunk in range(4):
@@ -353,8 +365,9 @@
             + self.recv_full[slot, 1].astype(f32)
         )
 
-    def begin(self):
-        for push in (self.far, self.near):
+    def begin(self, late=False):
+        self.late = late
+        for push in (self.far,) if late else (self.far, self.near):
             for chunk in range(4):
                 for kind in range(2):
                     push(kind, 1, chunk)
@@ -363,6 +376,9 @@
         for kind in range(2):
             for side in range(2):
                 self.middle(kind, 1, chunk, side)
+        if self.late:
+            for kind in range(2):
+                self.near(kind, 1, chunk)
 
     def step2(self, chunk):
         for kind in range(2):
@@ -370,21 +386,46 @@
             self.sums[pl.ds((kind * 4 + chunk) * 32, 32), :] = total.astype(bf16)
 
     def step3(self):
-        for push in (self.far, self.near):
-            for kind in range(2):
-                push(kind, 0, 0)
-
-    def step4(self):
-        for kind in (1, 0):
+        for kind in range(2):
+            slot = self.slot(kind, 0, 0)
             for side in range(2):
-                self.middle(kind, 0, 0, side)
+                step = 1 if side == 0 else -1
+                _, whole, _ = self.source(kind, 0, 0, step)
+                self.push(
+                    self.sums.at[whole],
+                    self.recv_full.at[slot, side],
+                    slot * 6 + 2 + side,
+                    self.along(kind, 0, step),
+                )
+            _, _, halves = self.source(kind, 0, 0, 2)
+            for side in range(2):
+                self.push(
+                    self.sums.at[halves[side]],
+                    self.recv_half.at[slot, side],
+                    slot * 6 + side,
+                    self.along(kind, 0, 2),
+                )
+
+    def sum0(self, kind):
+        slot = self.slot(kind, 0, 0)
+        for side in range(2):
+            self.arrived(self.recv_full.at[slot, side], slot * 6 + 2 + side)
+            self.arrived(self.recv_half.at[slot, side], slot * 6 + side)
+        _, whole, _ = self.source(kind, 0, 0, 0)
+        far = jnp.concatenate([self.recv_half[slot, 0], self.recv_half[slot, 1]], axis=0)
+        return (
+            self.sums[whole, :].astype(f32)
+            + self.recv_full[slot, 0].astype(f32)
+            + self.recv_full[slot, 1].astype(f32)
+            + far.astype(f32)
+        )
 
     def step5(self):
-        self.last[0] = self.total(1, 0, 0).astype(bf16)
+        self.last[0] = self.sum0(1).astype(bf16)
         self.push(self.last.at[0], self.last.at[1], 60, self.me.dp_device(dh=1))
 
     def result(self):
-        own = self.total(0, 0, 0)
+        own = self.sum0(0)
         self.arrived(self.last.at[1], 60)
         return own + self.last[1].astype(f32)
 
@@ -612,7 +653,7 @@
     def plane_devices(self):
         return [self.me.dp_device(dz=step // 4, dy=step % 4) for step in range(1, 16)]
 
-    def exchange(self, slots, place, value, devices, base):
+    def send_out(self, slots, place, value, devices, base):
         slots[place] = value
         for step, device in enumerate(devices):
             copy = remote(
@@ -620,6 +661,8 @@
             )
             copy.start()
             self.started.append(copy)
+
+    def add_up(self, slots, place, devices, base):
         for step, device in enumerate(devices):
             remote(
                 slots.at[place], slots.at[place], self.send, self.recv, base + step, device
@@ -629,10 +672,18 @@
             total = total + slots[slot]
         return total
 
-    def run(self, value):
+    def begin(self, value):
         me = self.me
-        value = self.exchange(self.row, me.h * 4 + me.t, value, self.row_devices(), 0)
-        value = self.exchange(self.plane, me.z * 4 + me.y, value, self.plane_devices(), 7)
+        self.send_out(self.row, me.h * 4 + me.t, value, self.row_devices(), 0)
+
+    def middle(self):
+        me = self.me
+        value = self.add_up(self.row, me.h * 4 + me.t, self.row_devices(), 0)
+        self.send_out(self.plane, me.z * 4 + me.y, value, self.plane_devices(), 7)
+
+    def result(self):
+        me = self.me
+        value = self.add_up(self.plane, me.z * 4 + me.y, self.plane_devices(), 7)
         for copy in self.started:
             copy.wait_send()
         return value
@@ -653,16 +704,7 @@
 
 
 def gather_services(gather):
-    steps = [gather.step1]
-    for kind in range(2):
-        for side in range(2):
-
-            def hand_on(kind=kind, side=side):
-                gather.pass_on(kind, 0, 0, side)
-                gather.spread(kind, 1, 1 + side)
-
-            steps.append(hand_on)
-    steps.append(gather.step3)
+    steps = [gather.step2, gather.step3]
     for chunk in range(4):
 
         def hand_bulk(chunk=chunk):
@@ -729,7 +771,6 @@
     for chunk in range(4):
         steps.append(functools.partial(scatter.step2, chunk))
     steps.append(scatter.step3)
-    steps.append(scatter.step4)
     steps.append(scatter.step5)
     return steps
 
@@ -771,14 +812,15 @@
     first = TokenScatter(me, part, *buffers)
     third = TokenScatter(me, part, *buffers)
     last = TokenScatter(me, ffn_part, *take(5))
-    attn = WeightGather(me, attn_full, *take(2))
-    ffn = WeightGather(me, ffn_full, *take(2))
+    attn = WeightGather(me, attn_full, True, *take(2))
+    ffn = WeightGather(me, ffn_full, False, *take(2))
     tokens = TokenGather(me, normed_ref, *take(2))
     upstream = TokenGather(me, grad_rows, *take(2))
     second = TokenGather(me, rows_ref, *take(2))
     back = TokenGather(me, back_rows, *take(2))
     attn_grad = grad_rows_t.at[:, pl.ds(0, 768)]
-    ffn_grad = GradScatter(me, ffn_full, *take(6))
+    down_grad = GradScatter(me, ffn_full.at[:, pl.ds(2304, 1152)], *take(6))
+    gate_grad = GradScatter(me, ffn_full.at[:, pl.ds(0, 2304)], *take(6))
     weight_grad = GradScatter(me, attn_grad, *take(6))
     gains = GainSum(me, *take(4))
     middle_grad = input_grad_ref
@@ -815,17 +857,18 @@
     attn.step3()
     attn.step4()
     ffn.begin()
-    for chunk in range(4):
-        tokens.pass_on(chunk)
-    tokens.finish()
-    attn.finish()
-    services = gather_services(ffn)
+    services = [ffn.step1] + [functools.partial(ffn.hand_on, kind, number) for kind in range(2) for number in range(2)]
+    services += gather_services(ffn)[1:]
 
     def serve(count=1):
         for _ in range(count):
             if services:
                 services.pop(0)()
 
+    for chunk in range(4):
+        tokens.pass_on(chunk)
+    tokens.finish()
+    attn.finish()
     serve()
     for chunk in range(4):
         upstream.begin(chunk)
@@ -911,18 +954,23 @@
     for chunk in range(4):
         first.begin_near(chunk)
 
-    def weight_tile(tile):
+    @pl.loop(0, 4)
+    def _(tile):
+        here = pl.ds(pl.multiple_of(tile * 256, 256), 256)
+        ffn_full[here, 2304:3456] = dot(grad_rows_t[here, :], activation[...]).astype(bf16)
+
+    down_grad.begin()
+    for chunk in range(4):
+        first.relay_on(chunk)
+
+    @pl.loop(0, 4)
+    def _(tile):
         here = pl.ds(pl.multiple_of(tile * 256, 256), 256)
         rows_t = turn(rows_ref[:, here])
         ffn_full[here, 0:1152] = dot(rows_t, gate_low[...]).astype(bf16)
         ffn_full[here, 1152:2304] = dot(rows_t, up_low[...]).astype(bf16)
-        ffn_full[here, 2304:3456] = dot(grad_rows_t[here, :], activation[...]).astype(bf16)
-
-    pl.loop(0, 1)(weight_tile)
-    for chunk in range(4):
-        first.relay_on(chunk)
-    pl.loop(1, 4)(weight_tile)
-    ffn_grad.begin()
+
+    gate_grad.begin(late=True)
     ffn_gain_total = jnp.zeros((1, 1024), f32)
     for chunk in range(4):
         here = pl.ds(chunk * 64, 64)
@@ -941,13 +989,17 @@
         last.begin_far(chunk)
     for chunk in range(4):
         last.begin_near(chunk)
-    services.extend(scatter_services(ffn_grad))
-    serve(3)
+    down_steps = scatter_services(down_grad)
+    gate_steps = scatter_services(gate_grad)
+    services.extend(down_steps[0:4])
+    serve(4)
+    services.extend(gate_steps[0:4] + down_steps[4:9])
     for chunk in range(4):
         back.pass_on(chunk)
+        if chunk >= 2:
+            serve(2)
     for chunk in range(4):
         last.relay_on(chunk)
-    serve(1)
     back.finish()
 
     @pl.loop(0, 4)
@@ -960,11 +1012,18 @@
         here = pl.ds(pl.multiple_of(tile * 256, 256), 256)
         attn_grad[here, 512:768] = dot(mixed_ref[...].astype(bf16), back_rows[:, here]).T.astype(bf16)
 
+    services.extend(gate_steps[4:8] + down_steps[9:10] + gate_steps[8:10])
     for number in range(4):
         for head in range(2):
             backward_block(low, head, number, acc)
-            if number == 3:
-                serve()
+            if number == 0:
+                serve(2)
+            if (number, head) == (1, 0):
+                serve(1)
+            if (number, head) in ((2, 0), (2, 1)):
+                serve(2)
+            if (number, head) == (3, 0):
+                serve(2)
     for chunk in range(4):
         here = pl.ds(chunk * 64, 64)
         out_ref[here, :] = (middle[here, :] + last.total(chunk)).astype(bf16)
@@ -975,7 +1034,7 @@
         q_part = q_part + q_more
         k_part = k_part + k_more
 
-    serve(2)
+    serve(1)
 
     def first_part(dx, dc):
         here = pl.ds(pl.multiple_of(me.token_block(dx, dc) * 256, 256), 256)
@@ -984,9 +1043,6 @@
     first_part(1, 1)
     for chunk in range(4):
         third.begin_far(chunk)
-    first_part(1, 0)
-    for chunk in range(4):
-        third.relay_on(chunk)
 
     @pl.loop(0, 4)
     def _(tile):
@@ -994,6 +1050,9 @@
         attn_grad[here, 0:512] = dot(turned[...], normed_ref[:, here]).T.astype(bf16)
 
     weight_grad.begin()
+    first_part(1, 0)
+    for chunk in range(4):
+        third.relay_on(chunk)
     first_part(0, 1)
     for chunk in range(4):
         third.begin_near(chunk)
@@ -1001,9 +1060,12 @@
     gain_rows[16:24, :] = jnp.zeros((8, 128), f32)
     gain_rows[16:17, 0:64] = jnp.broadcast_to(q_part, (64, 128)).T[0:1, :]
     gain_rows[17:18, 0:64] = jnp.broadcast_to(k_part, (64, 128)).T[0:1, :]
+    for chunk in range(4):
+        weight_grad.step1(chunk)
+    for chunk in range(4):
+        weight_grad.step2(chunk)
+    weight_grad.step3()
     serve(20)
-    for chunk in range(4):
-        weight_grad.step1(chunk)
     gain_total = jnp.zeros((1, 1024), f32)
     for chunk in range(4):
         here = pl.ds(chunk * 64, 64)
@@ -1018,15 +1080,14 @@
         lanes = slice(128 * part_number, 128 * part_number + 128)
         gain_rows[part_number : part_number + 1, :] = gain_total[:, lanes]
         gain_rows[8 + part_number : 9 + part_number, :] = ffn_gain_total[:, lanes]
-    for chunk in range(4):
-        weight_grad.step2(chunk)
-    weight_grad.step3()
-    gains_ref[...] = gains.run(gain_rows[...])
-    weight_grad.step4()
+    gains.begin(gain_rows[...])
     weight_grad.step5()
-    ffn_shard_ref[...] = ffn_grad.result()
+    gains.middle()
+    ffn_shard_ref[:, 2304:3456] = down_grad.result()
+    ffn_shard_ref[:, 0:2304] = gate_grad.result()
     attn_shard_ref[...] = weight_grad.result()
-    for transfer in (third, last, ffn_grad, weight_grad):
+    gains_ref[...] = gains.result()
+    for transfer in (third, last, down_grad, gate_grad, weight_grad):
         transfer.finish()
 
 
@@ -1119,7 +1180,8 @@
         + scatter_scratch() * 2
         + sems(41) * 2
         + sems(12) * 4
-        + grad_scratch(3456)
+        + grad_scratch(1152)
+        + grad_scratch(2304)
         + grad_scratch(768)
         + gain_scratch(),
         0,

time: 177 us -> 171 us (0.966)
  Pallas kernels: 176 us -> 170 us
    pallas_call x1, Pallas kernels: 173 us -> 167 us  [call(): pl.pallas_call(kernel, out_shape=outs, in_specs=[VMEM_SPEC] * len(args),...]
where the time goes in v2:
time: 171 us
  Pallas kernels  170 us (99%)
    pallas_call x1, Pallas kernels, call(): pl.pallas_call(kernel, out_shape=outs, in_specs=[VMEM_SPEC] * len(args),...  167 us

profile of v2, /device:TPU:0, one launch (start us, length us, event | category | flops | bytes accessed | tf_op | source)
XLA Modules:
  0.0 170.5 jit_solution(14450170534990725055)
XLA Ops:
  0.7 166.9 %shard_map.237 = (bf16[256,1024]{1,0:T(8,128)(2,1)}, f32[256,1024]{1,0:T(8,128)}, f32[32,768]{1,0:T(8,128)}, f32[32,3456]{1,0:T(8,128)}, f32[24,128]{1,0:T(8,128)}) custom-call(bf16[256,1024]{1,0:T(8,128)(2,1)} %x_ref.1, s32[1,1024]{1,0:T(1,128)} %bitcast.15, f32[1,1024]{1,0:T(1,128)} %bitcast.16, bf16[32,256]{1,0:T(8,128)(2,1)} %wq_ref.1, ...), custom_call_target="tpu_custom_call" | custom-call | tf_op jit(solution)/shard_map/pallas_call | solution.py:459
  167.5 2.9 %shard_map.238 = (bf16[256,1024]{1,0:T(8,128)(2,1)}, f32[256,1024]{1,0:T(8,128)}, f32[1,1024]{1,0:T(1,128)}, f32[32,256]{1,0:T(8,128)}, f32[32,128]{1,0:T(8,128)...) custom-call(bf16[256,1024]{1,0:T(8,128)(2,1)} %get-tuple-element.31., ...), custom_call_target="tpu_custom_call" | custom-call | tf_op jit(solution)/shard_map/pallas_call | solution.py:1193
